TPU v7x, 256 devices: a whole 4x4x8 slice. The times are simulated.
256 devices in a mesh: ctx: 64 (over y, z, core), head: 4 (over x).
Axes of the slice: x: 4, y: 4, z: 8, core: 2. Of those that a mesh axis runs over, the one named last changes fastest.
Arguments:
- tokens: bfloat16 [32768, 4096], P('ctx', 'head'), may hold values from -16 to 16
- w_query: bfloat16 [4096, 2048], P(None, 'head'), as said below
- w_key: bfloat16 [4096, 2048], P(None, 'head'), as said below
- w_value: bfloat16 [4096, 2048], P(None, 'head'), as said below
- gate_logit: float32 [16], P('head'), may hold values from -1 to 3
Outputs:
- attended: bfloat16 [32768, 2048], P('ctx', 'head')
Inputs may be any that keep to these rules, and one draw needn't show every extreme that they name: `w_query`: entries of order 4096 ** -0.5. `w_key`: entries of order 4096 ** -0.5. `w_value`: entries of order 4096 ** -0.5.
All inputs are finite; a program needn't handle non-finite values.
Results may differ from a plain program's by a relative error of at most 0.0098.
Values may be sent and summed in bfloat16 or wider, within the bound.
A program may use at most 128 MiB of HBM per device.

v0:
```python
import math

import jax
import jax.numpy as jnp
from jax import lax
from jax.sharding import PartitionSpec as P

HD = 128


def feature_map(inputs_arr):
    return jax.nn.elu(inputs_arr) + 1.0


def per_device(tokens, w_query, w_key, w_value, gate_logit):
    tok_rows = tokens.shape[0]
    width = w_query.shape[1]
    heads_here = width // HD
    column_piece = lax.all_gather(tokens, "head", axis=1, tiled=True)
    projected = tuple(
        (
            jnp.dot(column_piece, weight, preferred_element_type=jnp.float32)
            for weight in (w_query, w_key, w_value)
        )
    )
    queries, key_rows, values = (
        block.astype(jnp.bfloat16).reshape(tok_rows, heads_here, HD) for block in projected
    )
    mapped_keys = feature_map(key_rows.astype(jnp.float32)).astype(jnp.bfloat16)
    update = jnp.einsum("thd,the->hde", mapped_keys, values, preferred_element_type=jnp.float32)
    norm_update = jnp.sum(mapped_keys.astype(jnp.float32), axis=0)
    own_index = lax.axis_index("ctx")
    shard_piece = (
        lax.all_gather(update[None].astype(jnp.bfloat16), "ctx", axis=0, tiled=True).astype(
            jnp.float32
        ),
        lax.all_gather(norm_update[None].astype(jnp.bfloat16), "ctx", axis=0, tiled=True).astype(
            jnp.float32
        ),
    )
    row_count = shard_piece[0].shape[0]
    earlier_mask = (jnp.arange(row_count) < own_index).astype(jnp.float32)
    new_memory = jnp.zeros_like(update) + jnp.tensordot(
        earlier_mask, shard_piece[0], axes=1, precision=lax.Precision.HIGHEST
    )
    new_norm = jnp.zeros_like(norm_update) + jnp.tensordot(
        earlier_mask, shard_piece[1], axes=1, precision=lax.Precision.HIGHEST
    )
    mapped_query = feature_map(queries.astype(jnp.float32))
    numerator = jnp.einsum(
        "thd,hde->the", mapped_query, new_memory, precision=lax.Precision.HIGHEST
    )
    denominator = jnp.einsum("thd,hd->th", mapped_query, new_norm, precision=lax.Precision.HIGHEST)
    retrieved = numerator / jnp.maximum(denominator, 1.0)[:, :, None]
    scores = jnp.einsum(
        "thd,uhd->htu", queries, key_rows, preferred_element_type=jnp.float32
    ) / math.sqrt(HD)
    causal = jnp.arange(tok_rows)[:, None] >= jnp.arange(tok_rows)[None, :]
    scores = jnp.where(causal[None], scores, -jnp.inf)
    row_max = jnp.max(scores, axis=-1, keepdims=True)
    weights = jnp.exp(scores - row_max)
    probs = (weights / jnp.sum(weights, axis=-1, keepdims=True)).astype(jnp.bfloat16)
    local_part = jnp.einsum("htu,uhd->thd", probs, values, preferred_element_type=jnp.float32)
    gate_share = jax.nn.sigmoid(gate_logit)
    mixed = gate_share[None, :, None] * retrieved + (1.0 - gate_share)[None, :, None] * local_part
    return mixed.astype(jnp.bfloat16).reshape(tok_rows, width)


def solution(mesh):
    return jax.shard_map(
        per_device,
        mesh=mesh,
        in_specs=(P("ctx", "head"), P(None, "head"), P(None, "head"), P(None, "head"), P("head")),
        out_specs=P("ctx", "head"),
        check_vma=False,
    )
```

profile of v0, /device:TPU:1, one launch (start us, length us, event | category | flops | bytes accessed | tf_op | source)
XLA Modules:
  0.0 179.0 jit_solution(17159683463033878723)
XLA Ops:
  6.5 0.0 all-gather.4.cloned.1.call-start
  6.5 0.7 all-gather.4.cloned.1.call-update
  7.3 0.0 all-gather.6.cloned.1.call-start
  7.3 56.5 %all-gather.4.cloned.1.call-done = bf16[512,4096]{1,0:T(8,128)(2,1)} async-done(((bf16[512,1024]{1,0:T(8,128)(2,1)}), bf16[512,4096]{1,0:T(8,128)(2,1)}) %all-gather.4.cloned.1.call-update) | async-done | bytes 4194320 | tf_op jit(solution)/shard_map/all_gather | solution.py:19
  63.8 6.3 %fusion.32 = (bf16[512]{0:T(512)(128)(2,1)S(1)}, bf16[512,512]{0,1:T(8,128)(2,1)S(1)}) fusion(bf16[512,4096]{1,0:T(8,128)(2,1)} %all-gather.4.cloned.1.call-done, bf16[4096,512]{1,0:T(8,128)(2,1)} %param.7), kind=kOutput, calls=%fused_computation.45 | convolution fusion | flops 2149580288 | bytes 8913920 | tf_op jit(solution)/shard_map/dot_general | solution.py:22
  70.0 0.3 copy.14
  70.3 0.0 copy-start
  70.3 5.8 %convolution_convert_fusion.1 = bf16[512,512]{0,1:T(8,128)(2,1)S(1)} fusion(bf16[512,4096]{1,0:T(8,128)(2,1)} %all-gather.4.cloned.1.call-done, bf16[4096,512]{1,0:T(8,128)(2,1)} %param.8), kind=kOutput, calls=%fused_computation.24 | convolution fusion | flops 2147745792 | bytes 8912896 | tf_op jit(solution)/shard_map/dot_general | solution.py:22
  76.2 1.3 convolution_convert_fusion.3
  77.5 0.0 all-gather.6.cloned.1.call-update
  77.5 0.1 iota_compare_fusion
  77.6 0.0 copy-done
  77.7 5.8 %convolution_convert_fusion = bf16[512,512]{0,1:T(8,128)(2,1)S(1)} fusion(bf16[512,4096]{1,0:T(8,128)(2,1)} %all-gather.4.cloned.1.call-done, bf16[4096,512]{1,0:T(8,128)(2,1)} %param.6), kind=kOutput, calls=%fused_computation.23 | convolution fusion | flops 2147745792 | bytes 8912896 | tf_op jit(solution)/shard_map/dot_general | solution.py:22
  83.5 0.3 copy.17
  83.8 45.4 %all_gather.11 = bf16[64,4,128]{2,1,0:T(4,128)(2,1)S(1)} all-gather(bf16[1,4,128]{2,1,0:T(4,128)(2,1)S(1)} %bitcast.61), channel_id=1, replica_groups=mesh['ctx'=64,'head'=4] {'ctx'}, dimensions={0}, use_global_device_ids=true | all-gather | bytes 66560 | tf_op jit(solution)/shard_map/all_gather | solution.py:37
  129.2 0.1 convolution_bitcast_fusion.1
  129.3 1.3 fusion.22
  130.6 3.6 %fusion.53 = (f32[4,512]{1,0:T(4,128)S(1)}, f32[4,512,512]{1,2,0:T(8,128)}) fusion(pred[512,512]{0,1:T(8,128)(4,1)S(1)} %iota_compare_fusion, bf16[512,4,128]{0,2,1:T(8,128)(2,1)S(1)} %bitcast.58, bf16[512,4,128]{0,2,1:T(8,128)(2,1)S(1)} %bitcast.56), kind=kOutput, calls=%fused_computation.68 | convolution fusion | flops 272630272 | bytes 5513216 | tf_op jit(solution)/shard_map/sub | solution.py:61
  134.3 2.8 %fusion.12 = f32[512,4,128]{0,2,1:T(8,128)S(1)} fusion(bf16[512,4,128]{0,2,1:T(8,128)(2,1)S(1)} %bitcast.63, f32[4,512,512]{1,2,0:T(8,128)} %get-tuple-element.8, f32[4,512]{1,0:T(4,128)S(1)} %get-tuple-element.7, f32[4]{0:T(128)S(1)} %get-tuple-element.5), kind=kOutput, calls=%fused_computation.22 | convolution fusion | flops 270794752 | bytes 5775376 | tf_op jit(solution)/shard_map/htu,uhd->thd/dot_general | solution.py:63
  137.1 24.5 %all-gather.6.cloned.1.call-done = bf16[256,128,128]{2,1,0:T(8,128)(2,1)} async-done(((bf16[4,128,128]{2,1,0:T(8,128)(2,1)}), bf16[256,128,128]{2,1,0:T(8,128)(2,1)}) %all-gather.6.cloned.1.call-update) | async-done | bytes 8388624 | tf_op jit(solution)/shard_map/all_gather | solution.py:34
  161.6 8.0 %fusion.1 = f32[1,4,128,128]{3,0,2,1:T(1,128)S(1)} fusion(bf16[64,4,128,128]{3,2,1,0:T(8,128)(2,1)} %bitcast.54, s32[]{:T(128)S(6)} %axis_index.15), kind=kOutput, calls=%fused_computation.1 | convolution fusion | flops 8388672 | bytes 8650756 | tf_op jit(solution)/shard_map/dot_general | solution.py:43
  169.6 1.6 fusion.13
  171.1 1.0 copy.21
  (2 shorter events, 0.0 us)
Async XLA Ops:
  6.5 57.2 %all-gather.4.cloned.1.call-start = ((), (), s32[]{:S(2)}) async-start(), calls=%async_computation | async-start | bytes 5242880 | tf_op jit(solution)/shard_map/all_gather | solution.py:19
  7.3 154.4 %all-gather.6.cloned.1.call-start = ((), (), s32[]{:S(2)}) async-start(), calls=%async_computation.1 | async-start | bytes 8519680 | tf_op jit(solution)/shard_map/all_gather | solution.py:34
  70.3 7.3 %copy-start = (f32[4]{0:T(128)S(1)}, f32[4]{0:T(128)}, u32[]{:S(2)}) copy-start(f32[4]{0:T(128)} %param.9) | copy-start | bytes 52
Sparse Core Ops, SparseCore 0:
  9.2 54.5 all-gather.3
  77.7 83.9 all-gather.5
where the time goes:
time: 179 us
  waiting for transfers between devices  81.7 us (46%)
  blocking collectives  45.4 us (25%)
  matrix products  36.7 us (21%)
  between operations  13.5 us (8%)
    all_gather x1, waiting for transfers between devices, per_device(): column_piece = lax.all_gather(tokens, 'head', axis=1, tiled=True)  56.5 us
    all_gather x1, blocking collectives, per_device(): lax.all_gather(norm_update[None].astype(jnp.bfloat16), 'ctx', axis=0, til...  45.4 us
    all_gather x1, waiting for transfers between devices, per_device(): lax.all_gather(update[None].astype(jnp.bfloat16), 'ctx', axis=0, tiled=True)  24.5 us
    dot_general x3, matrix products, per_device(): jnp.dot(column_piece, weight, preferred_element_type=jnp.float32)  17.9 us
    dot_general x1, matrix products, per_device(): jnp.tensordot(earlier_mask, shard_piece[0], axes=1, precision=lax.Precisi...  7.97 us
    sub x1, matrix products, per_device(): weights = jnp.exp(scores - row_max)  3.63 us
  transfers between devices with their start and end apart: 2, of which 2 were waited for; matrix products, arithmetic and copies ran while one was open for 8% of the time, Pallas kernels for 0%

commit v1 on v0

v1 whole, which is shorter than its diff:
```python
import functools
import math

import jax
import jax.numpy as jnp
from jax import lax
from jax.experimental import pallas as pl
from jax.experimental.pallas import tpu as pltpu
from jax.sharding import PartitionSpec as P

MESH = pl.DeviceIdType.MESH
F32, BF16 = jnp.float32, jnp.bfloat16
HD = 128
TOK = 512
WIDTH = 512
DEPTH = 1024
HEADS = 4
ROWDEV = 16
YS = 4
SLICE = 32
MSG = 48
CHUNKS = ((0, 128), (128, 128), (256, 128), (384, 128))
AHEAD = 2
FAR_FIRST = (8, 7, 9, 6, 10, 5, 11, 4, 12, 3, 13, 2, 14, 1, 15)


def phi(u):
    return jnp.where(u > 0, u + 1.0, jnp.exp(jnp.minimum(u, 0.0)))


def dot(a, b):
    return jnp.dot(a, b, preferred_element_type=F32)


def kernel(
    tok_hbm, wq_hbm, wk_hbm, wv_hbm, gate_ref, out_ref,
    tok, weights, qkv, acc, update, norm, mapped_q, local, scale,
    send1, got1, send2, got2, prefix, send3, memory,
    load_sem, x_send, x_recv, s_send, s_recv,
):
    me = lax.axis_index("ctx")
    x = lax.axis_index("head")
    col, row = lax.rem(me, ROWDEV), me // ROWDEV
    right, left = {"head": lax.rem(x + 1, 4)}, {"head": lax.rem(x + 3, 4)}
    sides = (right, left)

    def in_row(d):
        return {"ctx": row * ROWDEV + lax.rem(col + d, ROWDEV)}

    def in_column(d):
        return {"ctx": lax.rem(row + d, YS) * ROWDEV + col}

    loads = [pltpu.make_async_copy(tok_hbm, tok.at[0], load_sem.at[0])]
    for p, w in enumerate((wq_hbm, wk_hbm, wv_hbm)):
        loads.append(pltpu.make_async_copy(w, weights.at[p], load_sem.at[1 + p]))
    for load in loads:
        load.start()

    barrier = pltpu.get_barrier_semaphore()
    partners = [in_row(d) for d in FAR_FIRST] + [in_column(d) for d in (2, 1, 3)] + [right, left]
    for target in partners:
        pl.semaphore_signal(barrier, inc=1, device_id=target, device_id_type=MESH)
    pl.semaphore_wait(barrier, len(partners))

    def own(c, j):
        rows = pl.ds(*CHUNKS[c])
        return pltpu.make_async_remote_copy(
            src_ref=tok_hbm.at[rows], dst_ref=tok.at[1 + j, rows],
            send_sem=x_send.at[j, c], recv_sem=x_recv.at[j, c],
            device_id=sides[j], device_id_type=MESH,
        )

    def forward(c, j):
        first, count = CHUNKS[c]
        rows = pl.ds(first + j * (count // 2), count // 2)
        return pltpu.make_async_remote_copy(
            src_ref=tok.at[1 + j, rows], dst_ref=tok.at[3, rows],
            send_sem=x_send.at[2 + j, c], recv_sem=x_recv.at[2 + j, c],
            device_id=sides[j], device_id_type=MESH,
        )

    sources = (x, lax.rem(x + 3, 4), lax.rem(x + 1, 4), lax.rem(x + 2, 4))

    def partial_sum(p, c, which):
        rows = pl.ds(*CHUNKS[c])
        return sum(dot(tok[s, rows, :], weights[p, sources[s]]) for s in which)

    def keep(p, c, total):
        total = total.astype(BF16)
        for h in range(HEADS):
            qkv[p, h, pl.ds(*CHUNKS[c]), :] = total[:, h * HD : (h + 1) * HD]

    def add_update(c):
        rows = pl.ds(*CHUNKS[c])

        def head(h, carry):
            mapped = phi(qkv[1, h, rows, :].astype(F32)).astype(BF16)
            new = lax.dot_general(
                mapped, qkv[2, h, rows, :], (((0,), (0,)), ((), ())), preferred_element_type=F32
            )
            new_norm = dot(jnp.ones((16, CHUNKS[c][1]), BF16), mapped)
            if c == 0:
                update[h] = new
                norm[h] = new_norm
            else:
                update[h] += new
                norm[h] += new_norm
            return carry

        lax.fori_loop(0, HEADS, head, 0)

    last = len(CHUNKS) - 1
    for c in range(AHEAD):
        for j in range(2):
            own(c, j).start()
    for load in loads:
        load.wait()
    for c in range(last + 1):
        for j in range(2):
            own(c, j).wait_recv()
            forward(c, j).start()
        if c + AHEAD <= last:
            for j in range(2):
                own(c + AHEAD, j).start()
        if c > 0:
            for j in range(2):
                forward(c - 1, j).wait_recv()

            def project(p, carry, c=c):
                keep(p, c - 1, partial_sum(p, c - 1, (0, 1, 2, 3)))
                return carry

            lax.fori_loop(0, 3, project, 0)
            add_update(c - 1)

    def begin(p, carry):
        acc[p] = partial_sum(p, last, (0, 1, 2))
        return carry

    lax.fori_loop(0, 3, begin, 0)
    for j in range(2):
        forward(last, j).wait_recv()

    def finish(p, carry):
        keep(p, last, acc[p] + partial_sum(p, last, (3,)))
        return carry

    lax.fori_loop(1, 3, finish, 0)
    add_update(last)

    tile_row = lax.broadcasted_iota(jnp.int32, (16, HD), 0)
    tile = jnp.zeros((16, HD), F32)
    for h in range(HEADS):
        high = norm[h].astype(BF16).astype(F32)
        tile = jnp.where(tile_row == h, high, tile)
        tile = jnp.where(tile_row == HEADS + h, norm[h] - high, tile)
    tile = tile.astype(BF16)
    for h in range(HEADS):
        send1[4 * h : 4 * h + 4, 0:SLICE, :] = update[h].reshape(4, SLICE, HD).astype(BF16)
    for d in range(ROWDEV):
        send1[d, SLICE:MSG, :] = tile

    def exchange(step, src, dst):
        for d in FAR_FIRST:
            pltpu.make_async_remote_copy(
                src_ref=src.at[lax.rem(col + d, ROWDEV)], dst_ref=dst.at[col],
                send_sem=s_send.at[step], recv_sem=s_recv.at[step],
                device_id=in_row(d), device_id_type=MESH,
            ).start()
        dst[col] = src[col]

    def all_of(step, src, dst, count):
        return pltpu.make_async_remote_copy(
            src_ref=src.at[pl.ds(0, count)], dst_ref=dst.at[pl.ds(0, count)],
            send_sem=s_send.at[step], recv_sem=s_recv.at[step],
            device_id=right, device_id_type=MESH,
        )

    def attend(h, carry):
        q, k, v = qkv.at[0, h], qkv.at[1, h], qkv.at[2, h]
        mapped_q[h] = phi(q[...].astype(F32)).astype(BF16)
        share = jax.nn.sigmoid(jnp.full((8, HD), gate_ref[h], F32))[0:1, :]
        for i in range(4):
            mine, seen = pl.ds(i * 128, 128), (i + 1) * 128
            scores = lax.dot_general(
                q[mine, :], k[0:seen, :], (((1,), (1,)), ((), ())), preferred_element_type=F32
            ) * (1.0 / math.sqrt(HD))
            at = lax.broadcasted_iota(jnp.int32, (128, seen), 0) + i * 128
            of = lax.broadcasted_iota(jnp.int32, (128, seen), 1)
            scores = jnp.where(of <= at, scores, -jnp.inf)
            w = jnp.exp(scores - jnp.max(scores, axis=-1, keepdims=True))
            probs = (w / jnp.sum(w, axis=-1, keepdims=True)).astype(BF16)
            local[h, mine, :] = (1.0 - share) * dot(probs, v[0:seen, :])
        return carry

    exchange(0, send1, got1)
    lax.fori_loop(0, 1, finish, 0)
    lax.fori_loop(0, 2, attend, 0)
    all_of(0, send1, got1, ROWDEV - 1).wait_recv()

    running = jnp.zeros((MSG, HD), F32)
    for s in range(ROWDEV):
        prefix[s] = running
        running = running + got1[s].astype(F32)
    send2[...] = running.astype(BF16)
    for d in (2, 1, 3):
        pltpu.make_async_remote_copy(
            src_ref=send2, dst_ref=got2.at[row], send_sem=s_send.at[1], recv_sem=s_recv.at[1],
            device_id=in_column(d), device_id_type=MESH,
        ).start()
    got2[row] = send2[...]
    lax.fori_loop(2, 3, attend, 0)
    all_of(1, got2, got2, YS - 1).wait_recv()

    offset = jnp.zeros((MSG, HD), F32)
    for r in range(YS):
        offset = offset + jnp.where(r < row, got2[r].astype(F32), 0.0)
    for s in range(ROWDEV):
        send3[s] = (prefix[s, 0:SLICE, :] + offset[0:SLICE, :]).astype(BF16)
    exchange(2, send3, memory)
    lax.fori_loop(3, 4, attend, 0)

    total_norm = prefix[col, SLICE:MSG, :] + offset[SLICE:MSG, :]
    for h in range(HEADS):
        normalizer = total_norm[h : h + 1, :] + total_norm[HEADS + h : HEADS + h + 1, :]
        share = jax.nn.sigmoid(jnp.full((8, HD), gate_ref[h], F32))[0:1, :]
        below = jnp.sum(mapped_q[h].astype(F32) * normalizer, axis=-1, keepdims=True)
        scale[h] = share / jnp.maximum(below, 1.0)
    all_of(2, send3, memory, ROWDEV - 1).wait_recv()

    for h in range(HEADS):
        held = memory[4 * h : 4 * h + 4].reshape(HD, HD)
        out_ref[:, h * HD : (h + 1) * HD] = (
            scale[h] * dot(mapped_q[h], held) + local[h]
        ).astype(BF16)

    for c in range(last + 1):
        for j in range(2):
            own(c, j).wait_send()
            forward(c, j).wait_send()
    all_of(0, send1, got1, ROWDEV - 1).wait_send()
    all_of(1, got2, got2, YS - 1).wait_send()
    all_of(2, send3, memory, ROWDEV - 1).wait_send()


def per_device(tokens, w_query, w_key, w_value, gate_logit):
    weights = tuple(w.reshape(4, DEPTH, WIDTH) for w in (w_query, w_key, w_value))
    anywhere = pl.BlockSpec(memory_space=pl.ANY)
    steps = len(CHUNKS)
    return pl.pallas_call(
        kernel,
        out_shape=jax.ShapeDtypeStruct((TOK, WIDTH), BF16),
        in_specs=[anywhere] * 4 + [pl.BlockSpec(memory_space=pltpu.SMEM)],
        out_specs=pl.BlockSpec(memory_space=pltpu.VMEM),
        scratch_shapes=[
            pltpu.VMEM((4, TOK, DEPTH), BF16),
            pltpu.VMEM((3, 4, DEPTH, WIDTH), BF16),
            pltpu.VMEM((3, HEADS, TOK, HD), BF16),
            pltpu.VMEM((3, CHUNKS[-1][1], WIDTH), F32),
            pltpu.VMEM((HEADS, HD, HD), F32),
            pltpu.VMEM((HEADS, 16, HD), F32),
            pltpu.VMEM((HEADS, TOK, HD), BF16),
            pltpu.VMEM((HEADS, TOK, HD), F32),
            pltpu.VMEM((HEADS, TOK, HD), F32),
            pltpu.VMEM((ROWDEV, MSG, HD), BF16),
            pltpu.VMEM((ROWDEV, MSG, HD), BF16),
            pltpu.VMEM((MSG, HD), BF16),
            pltpu.VMEM((YS, MSG, HD), BF16),
            pltpu.VMEM((ROWDEV, MSG, HD), F32),
            pltpu.VMEM((ROWDEV, SLICE, HD), BF16),
            pltpu.VMEM((ROWDEV, SLICE, HD), BF16),
            pltpu.SemaphoreType.DMA((4,)),
            pltpu.SemaphoreType.DMA((4, steps)),
            pltpu.SemaphoreType.DMA((4, steps)),
            pltpu.SemaphoreType.DMA((3,)),
            pltpu.SemaphoreType.DMA((3,)),
        ],
        compiler_params=pltpu.CompilerParams(
            collective_id=0, has_side_effects=True, vmem_limit_bytes=48 << 20
        ),
        cost_estimate=pl.CostEstimate(
            flops=7_400_000_000, bytes_accessed=15_000_000, transcendentals=2_000_000
        ),
    )(tokens, *weights, gate_logit)


def solution(mesh):
    return jax.shard_map(
        per_device,
        mesh=mesh,
        in_specs=(P("ctx", "head"), P(None, "head"), P(None, "head"), P(None, "head"), P("head")),
        out_specs=P("ctx", "head"),
        check_vma=False,
    )
```

time: 179 us -> 71.6 us (0.40)
  waiting for transfers between devices: 81.7 us -> 0 us
  Pallas kernels: 0 us -> 66.5 us
  blocking collectives: 45.4 us -> 0 us
  matrix products: 36.7 us -> 0 us
  between operations: 13.5 us -> 0.01 us
  local copies, waits for them, and re-layouts: 1.59 us -> 4.86 us
    all_gather x2 -> x0, waiting for transfers between devices: 81 us -> none  [the longest x1 56.5 us: per_device(): column_piece = lax.all_gather(tokens, 'head', axis=1, tiled=True)]
    pallas_call x0 -> x1, Pallas kernels: none -> 66.5 us  [per_device(): pl.pallas_call(kernel, out_shape=jax.ShapeDtypeStruct((TOK, WIDTH), BF16)...]
    all_gather x1 -> x0, blocking collectives: 45.4 us -> none  [per_device(): lax.all_gather(norm_update[None].astype(jnp.bfloat16), 'ctx', axis=0, til...]
    dot_general x9 -> x0, matrix products: 33 us -> none  [the longest x3 17.9 us: per_device(): jnp.dot(column_piece, weight, preferred_element_type=jnp.float32)]
    unnamed x2 -> x7, local copies, waits for them, and re-layouts: 0.01 us -> 4.86 us
    sub x1 -> x0, matrix products: 3.63 us -> none  [per_device(): weights = jnp.exp(scores - row_max)]
  transfers between devices with their start and end apart: 2 -> 0, of which waited for: 2 -> 0; matrix products, arithmetic and copies ran while one was open for 8% -> 0% of each run, Pallas kernels for 0% -> 0%
where the time goes in v1:
time: 71.6 us; the launch traced here: 71.4 us
  Pallas kernels  66.5 us (93%)
  local copies, waits for them, and re-layouts  4.86 us (7%)
    pallas_call x1, Pallas kernels, per_device(): pl.pallas_call(kernel, out_shape=jax.ShapeDtypeStruct((TOK, WIDTH), BF16)...  66.5 us
    unnamed x7, local copies, waits for them, and re-layouts  4.86 us

profile of v1, /device:TPU:1, one launch (start us, length us, event | category | flops | bytes accessed | tf_op | source)
XLA Modules:
  0.0 71.4 jit_solution(13908283412756064576)
XLA Ops:
  0.0 0.0 copy-start
  0.0 2.2 %copy-done = bf16[4096,512]{1,0:T(8,128)(2,1)S(1)} copy-done((bf16[4096,512]{1,0:T(8,128)(2,1)S(1)}, bf16[4096,512]{1,0:T(8,128)(2,1)}, u32[]{:S(2)}) %copy-start) | copy-done | bytes 4194328
  2.2 0.0 copy-start.1
  2.2 1.2 %copy-done.1 = bf16[512,1024]{1,0:T(8,128)(2,1)S(1)} copy-done((bf16[512,1024]{1,0:T(8,128)(2,1)S(1)}, bf16[512,1024]{1,0:T(8,128)(2,1)}, u32[]{:S(2)}) %copy-start.1) | copy-done | bytes 1048600
  3.4 0.0 copy-start.2
  3.4 0.7 copy-done.2
  4.1 66.5 %shard_map.55 = bf16[512,512]{1,0:T(8,128)(2,1)S(1)} custom-call(bf16[512,1024]{1,0:T(8,128)(2,1)S(1)} %copy-done.1, bf16[4,1024,512]{2,1,0:T(8,128)(2,1)S(1)} %bitcast.3, bf16[4,1024,512]{2,1,0:T(8,128)(2,1)} %bitcast.4, bf16[4,1024,512]{2,1,0:T(8,128)(2,1)} %bitcast.5, f32[4]{0:T(128)S(1)} %copy-done.2), custom_call_target="tpu_custom_call" | custom-call | flops 7400000000 | bytes 15000000 | tf_op jit(solution)/shard_map/pallas_call | solution.py:250
  70.6 0.8 %copy.7 = bf16[512,512]{1,0:T(8,128)(2,1)} copy(bf16[512,512]{1,0:T(8,128)(2,1)S(1)} %shard_map.55) | data formatting | bytes 1048576
Async XLA Ops:
  0.0 2.2 %copy-start = (bf16[4096,512]{1,0:T(8,128)(2,1)S(1)}, bf16[4096,512]{1,0:T(8,128)(2,1)}, u32[]{:S(2)}) copy-start(bf16[4096,512]{1,0:T(8,128)(2,1)} %param.6) | copy-start | bytes 12582916
  2.2 1.2 %copy-start.1 = (bf16[512,1024]{1,0:T(8,128)(2,1)S(1)}, bf16[512,1024]{1,0:T(8,128)(2,1)}, u32[]{:S(2)}) copy-start(bf16[512,1024]{1,0:T(8,128)(2,1)} %tok_hbm.1) | copy-start | bytes 3145732
  3.4 0.7 copy-start.2

commit v2 on v1

--- a/solution.py
+++ b/solution.py
@@ -19,8 +19,10 @@
 YS = 4
 SLICE = 32
 MSG = 48
-CHUNKS = ((0, 128), (128, 128), (256, 128), (384, 128))
+SIZES = (128, 128, 128, 128)
+CHUNKS = tuple((sum(SIZES[:i]), n) for i, n in enumerate(SIZES))
 AHEAD = 2
+DIRECT = 0
 FAR_FIRST = (8, 7, 9, 6, 10, 5, 11, 4, 12, 3, 13, 2, 14, 1, 15)
 
 
@@ -33,10 +35,10 @@
 
 
 def kernel(
-    tok_hbm, wq_hbm, wk_hbm, wv_hbm, gate_ref, out_ref,
-    tok, weights, qkv, acc, update, norm, mapped_q, local, scale,
+    tok_hbm, wq_hbm, wk_hbm, wv_hbm, gate_hbm, out_ref,
+    tok, weights, gate_ref, qkv, acc, update, norm, mapped_q, local, scale,
     send1, got1, send2, got2, prefix, send3, memory,
-    load_sem, x_send, x_recv, s_send, s_recv,
+    load_sem, x_send, x_recv, s_send, s_recv, met,
 ):
     me = lax.axis_index("ctx")
     x = lax.axis_index("head")
@@ -50,17 +52,28 @@
     def in_column(d):
         return {"ctx": lax.rem(row + d, YS) * ROWDEV + col}
 
-    loads = [pltpu.make_async_copy(tok_hbm, tok.at[0], load_sem.at[0])]
+    loads = [
+        pltpu.make_async_copy(tok_hbm, tok.at[0], load_sem.at[0]),
+        pltpu.make_async_copy(gate_hbm, gate_ref, load_sem.at[4]),
+    ]
     for p, w in enumerate((wq_hbm, wk_hbm, wv_hbm)):
         loads.append(pltpu.make_async_copy(w, weights.at[p], load_sem.at[1 + p]))
     for load in loads:
         load.start()
 
     barrier = pltpu.get_barrier_semaphore()
-    partners = [in_row(d) for d in FAR_FIRST] + [in_column(d) for d in (2, 1, 3)] + [right, left]
-    for target in partners:
+    near = [in_row(2), in_row(14), in_column(1), in_column(3)]
+    other = {"ctx": me + 1 - 2 * lax.rem(me, 2)}
+    for target in near + [other, right, left]:
         pl.semaphore_signal(barrier, inc=1, device_id=target, device_id_type=MESH)
-    pl.semaphore_wait(barrier, len(partners))
+    pl.semaphore_wait(barrier, len(near) + 3)
+
+    def meet(step):
+        for target in (near, [in_row(4), in_row(12)], [in_row(8)])[step]:
+            pl.semaphore_signal(met.at[step], inc=1, device_id=target, device_id_type=MESH)
+
+    def met_all(step):
+        pl.semaphore_wait(met.at[step], (4, 2, 1)[step])
 
     def own(c, j):
         rows = pl.ds(*CHUNKS[c])
@@ -69,6 +82,8 @@
             send_sem=x_send.at[j, c], recv_sem=x_recv.at[j, c],
             device_id=sides[j], device_id_type=MESH,
         )
+
+    last = len(CHUNKS) - 1
 
     def forward(c, j):
         first, count = CHUNKS[c]
@@ -78,6 +93,17 @@
             send_sem=x_send.at[2 + j, c], recv_sem=x_recv.at[2 + j, c],
             device_id=sides[j], device_id_type=MESH,
         )
+
+    def straight(c):
+        rows = pl.ds(*CHUNKS[c])
+        return pltpu.make_async_remote_copy(
+            src_ref=tok_hbm.at[rows], dst_ref=tok.at[3, rows],
+            send_sem=x_send.at[2, c], recv_sem=x_recv.at[2, c],
+            device_id={"head": lax.rem(x + 2, 4)}, device_id_type=MESH,
+        )
+
+    def to_opposite(c):
+        return [straight(c)] if c > last - DIRECT else [forward(c, 0), forward(c, 1)]
 
     sources = (x, lax.rem(x + 3, 4), lax.rem(x + 1, 4), lax.rem(x + 2, 4))
 
@@ -107,24 +133,33 @@
                 norm[h] += new_norm
             return carry
 
-        lax.fori_loop(0, HEADS, head, 0)
-
-    last = len(CHUNKS) - 1
-    for c in range(AHEAD):
+        lax.fori_loop(0, HEADS, head, 0, unroll=True)
+
+    def start_own(c):
         for j in range(2):
             own(c, j).start()
+        if c > last - DIRECT:
+            straight(c).start()
+
+    meet(0)
+    for c in range(AHEAD):
+        start_own(c)
     for load in loads:
         load.wait()
     for c in range(last + 1):
         for j in range(2):
             own(c, j).wait_recv()
-            forward(c, j).start()
+            if c <= last - DIRECT:
+                forward(c, j).start()
         if c + AHEAD <= last:
-            for j in range(2):
-                own(c + AHEAD, j).start()
+            start_own(c + AHEAD)
+        if c < 3:
+            met_all(c)
+            if c < 2:
+                meet(c + 1)
         if c > 0:
-            for j in range(2):
-                forward(c - 1, j).wait_recv()
+            for copy in to_opposite(c - 1):
+                copy.wait_recv()
 
             def project(p, carry, c=c):
                 keep(p, c - 1, partial_sum(p, c - 1, (0, 1, 2, 3)))
@@ -133,19 +168,12 @@
             lax.fori_loop(0, 3, project, 0)
             add_update(c - 1)
 
-    def begin(p, carry):
-        acc[p] = partial_sum(p, last, (0, 1, 2))
-        return carry
-
-    lax.fori_loop(0, 3, begin, 0)
-    for j in range(2):
-        forward(last, j).wait_recv()
-
-    def finish(p, carry):
-        keep(p, last, acc[p] + partial_sum(p, last, (3,)))
-        return carry
-
-    lax.fori_loop(1, 3, finish, 0)
+    for p in (1, 2):
+        acc[p - 1] = partial_sum(p, last, (0, 1, 2))
+    for copy in to_opposite(last):
+        copy.wait_recv()
+    for p in (1, 2):
+        keep(p, last, acc[p - 1] + partial_sum(p, last, (3,)))
     add_update(last)
 
     tile_row = lax.broadcasted_iota(jnp.int32, (16, HD), 0)
@@ -194,21 +222,24 @@
         return carry
 
     exchange(0, send1, got1)
-    lax.fori_loop(0, 1, finish, 0)
+    keep(0, last, partial_sum(0, last, (0, 1, 2, 3)))
     lax.fori_loop(0, 2, attend, 0)
     all_of(0, send1, got1, ROWDEV - 1).wait_recv()
 
-    running = jnp.zeros((MSG, HD), F32)
-    for s in range(ROWDEV):
-        prefix[s] = running
-        running = running + got1[s].astype(F32)
-    send2[...] = running.astype(BF16)
+    total = got1[0].astype(F32)
+    for s in range(1, ROWDEV):
+        total = total + got1[s].astype(F32)
+    send2[...] = total.astype(BF16)
     for d in (2, 1, 3):
         pltpu.make_async_remote_copy(
             src_ref=send2, dst_ref=got2.at[row], send_sem=s_send.at[1], recv_sem=s_recv.at[1],
             device_id=in_column(d), device_id_type=MESH,
         ).start()
     got2[row] = send2[...]
+    running = jnp.zeros((MSG, HD), F32)
+    for s in range(ROWDEV):
+        prefix[s] = running
+        running = running + got1[s].astype(F32)
     lax.fori_loop(2, 3, attend, 0)
     all_of(1, got2, got2, YS - 1).wait_recv()
 
@@ -237,7 +268,8 @@
     for c in range(last + 1):
         for j in range(2):
             own(c, j).wait_send()
-            forward(c, j).wait_send()
+        for copy in to_opposite(c):
+            copy.wait_send()
     all_of(0, send1, got1, ROWDEV - 1).wait_send()
     all_of(1, got2, got2, YS - 1).wait_send()
     all_of(2, send3, memory, ROWDEV - 1).wait_send()
@@ -250,13 +282,14 @@
     return pl.pallas_call(
         kernel,
         out_shape=jax.ShapeDtypeStruct((TOK, WIDTH), BF16),
-        in_specs=[anywhere] * 4 + [pl.BlockSpec(memory_space=pltpu.SMEM)],
+        in_specs=[anywhere] * 5,
         out_specs=pl.BlockSpec(memory_space=pltpu.VMEM),
         scratch_shapes=[
             pltpu.VMEM((4, TOK, DEPTH), BF16),
             pltpu.VMEM((3, 4, DEPTH, WIDTH), BF16),
+            pltpu.SMEM((HEADS,), F32),
             pltpu.VMEM((3, HEADS, TOK, HD), BF16),
-            pltpu.VMEM((3, CHUNKS[-1][1], WIDTH), F32),
+            pltpu.VMEM((2, CHUNKS[-1][1], WIDTH), F32),
             pltpu.VMEM((HEADS, HD, HD), F32),
             pltpu.VMEM((HEADS, 16, HD), F32),
             pltpu.VMEM((HEADS, TOK, HD), BF16),
@@ -269,14 +302,15 @@
             pltpu.VMEM((ROWDEV, MSG, HD), F32),
             pltpu.VMEM((ROWDEV, SLICE, HD), BF16),
             pltpu.VMEM((ROWDEV, SLICE, HD), BF16),
-            pltpu.SemaphoreType.DMA((4,)),
+            pltpu.SemaphoreType.DMA((5,)),
             pltpu.SemaphoreType.DMA((4, steps)),
             pltpu.SemaphoreType.DMA((4, steps)),
             pltpu.SemaphoreType.DMA((3,)),
             pltpu.SemaphoreType.DMA((3,)),
+            pltpu.SemaphoreType.REGULAR((3,)),
         ],
         compiler_params=pltpu.CompilerParams(
-            collective_id=0, has_side_effects=True, vmem_limit_bytes=48 << 20
+            collective_id=0, has_side_effects=True, vmem_limit_bytes=63 << 20
         ),
         cost_estimate=pl.CostEstimate(
             flops=7_400_000_000, bytes_accessed=15_000_000, transcendentals=2_000_000

time: 71.6 us -> 64.3 us (0.90)
  Pallas kernels: 66.5 us -> 62.3 us
  local copies, waits for them, and re-layouts: 4.86 us -> 1.87 us
    pallas_call x1, Pallas kernels: 66.5 us -> 62.3 us  [per_device(): pl.pallas_call(kernel, out_shape=jax.ShapeDtypeStruct((TOK, WIDTH), BF16)...]
    unnamed x7 -> x1, local copies, waits for them, and re-layouts: 4.86 us -> 1.87 us
where the time goes in v2:
time: 64.3 us; the launch traced here: 64.2 us
  Pallas kernels  62.3 us (97%)
  local copies, waits for them, and re-layouts  1.87 us (3%)
    pallas_call x1, Pallas kernels, per_device(): pl.pallas_call(kernel, out_shape=jax.ShapeDtypeStruct((TOK, WIDTH), BF16)...  62.3 us
    unnamed x1, local copies, waits for them, and re-layouts  1.87 us

profile of v2, /device:TPU:1, one launch (start us, length us, event | category | flops | bytes accessed | tf_op | source)
XLA Modules:
  0.0 64.2 jit_solution(13786474423362879604)
XLA Ops:
  0.0 62.3 %shard_map.55 = bf16[512,512]{1,0:T(8,128)(2,1)} custom-call(bf16[512,1024]{1,0:T(8,128)(2,1)} %tok_hbm.1, bf16[4,1024,512]{2,1,0:T(8,128)(2,1)} %bitcast.3, bf16[4,1024,512]{2,1,0:T(8,128)(2,1)} %bitcast.4, bf16[4,1024,512]{2,1,0:T(8,128)(2,1)} %bitcast.5, f32[4]{0:T(128)} %gate_hbm.1), custom_call_target="tpu_custom_call" | custom-call | flops 7400000000 | bytes 15000000 | tf_op jit(solution)/shard_map/pallas_call | solution.py:282
  62.3 1.9 %copy.7 = bf16[512,512]{1,0:T(8,128)(2,1)} copy(bf16[512,512]{1,0:T(8,128)(2,1)} %shard_map.55) | data formatting | bytes 1048576

commit v3 on v2

--- a/solution.py
+++ b/solution.py
@@ -18,12 +18,13 @@
 ROWDEV = 16
 YS = 4
 SLICE = 32
-MSG = 48
+TILE = 16
 SIZES = (128, 128, 128, 128)
 CHUNKS = tuple((sum(SIZES[:i]), n) for i, n in enumerate(SIZES))
 AHEAD = 2
 DIRECT = 0
 FAR_FIRST = (8, 7, 9, 6, 10, 5, 11, 4, 12, 3, 13, 2, 14, 1, 15)
+CHIPS_FAR_FIRST = (4, 3, 5, 2, 6, 1, 7)
 
 
 def phi(u):
@@ -37,12 +38,13 @@
 def kernel(
     tok_hbm, wq_hbm, wk_hbm, wv_hbm, gate_hbm, out_ref,
     tok, weights, gate_ref, qkv, acc, update, norm, mapped_q, local, scale,
-    send1, got1, send2, got2, prefix, send3, memory,
+    send1, got1, tile1, tiles1, send2, got2, tile2, tiles2, prefix, send3, memory,
     load_sem, x_send, x_recv, s_send, s_recv, met,
 ):
     me = lax.axis_index("ctx")
     x = lax.axis_index("head")
     col, row = lax.rem(me, ROWDEV), me // ROWDEV
+    chip, core = col // 2, lax.rem(col, 2)
     right, left = {"head": lax.rem(x + 1, 4)}, {"head": lax.rem(x + 3, 4)}
     sides = (right, left)
 
@@ -116,7 +118,7 @@
         for h in range(HEADS):
             qkv[p, h, pl.ds(*CHUNKS[c]), :] = total[:, h * HD : (h + 1) * HD]
 
-    def add_update(c):
+    def add_update(c, first=0, count=HEADS):
         rows = pl.ds(*CHUNKS[c])
 
         def head(h, carry):
@@ -124,7 +126,7 @@
             new = lax.dot_general(
                 mapped, qkv[2, h, rows, :], (((0,), (0,)), ((), ())), preferred_element_type=F32
             )
-            new_norm = dot(jnp.ones((16, CHUNKS[c][1]), BF16), mapped)
+            new_norm = dot(jnp.ones((TILE, CHUNKS[c][1]), BF16), mapped)
             if c == 0:
                 update[h] = new
                 norm[h] = new_norm
@@ -133,7 +135,7 @@
                 norm[h] += new_norm
             return carry
 
-        lax.fori_loop(0, HEADS, head, 0, unroll=True)
+        lax.fori_loop(first, first + count, head, 0, unroll=True)
 
     def start_own(c):
         for j in range(2):
@@ -172,30 +174,48 @@
         acc[p - 1] = partial_sum(p, last, (0, 1, 2))
     for copy in to_opposite(last):
         copy.wait_recv()
-    for p in (1, 2):
-        keep(p, last, acc[p - 1] + partial_sum(p, last, (3,)))
-    add_update(last)
-
-    tile_row = lax.broadcasted_iota(jnp.int32, (16, HD), 0)
-    tile = jnp.zeros((16, HD), F32)
+    mine = core * 8 + chip
+
+    def first_step(i, column):
+        return pltpu.make_async_remote_copy(
+            src_ref=send1.at[i], dst_ref=got1.at[col], send_sem=s_send.at[0], recv_sem=s_recv.at[0],
+            device_id={"ctx": row * ROWDEV + column}, device_id_type=MESH,
+        )
+
+    rows = pl.ds(*CHUNKS[last])
+    for half in range(2):
+        columns = pl.ds(half * 256, 256)
+        for p in (1, 2):
+            total = acc[p - 1, :, columns] + dot(tok[3, rows, :], weights[p, sources[3], :, columns])
+            total = total.astype(BF16)
+            for h in range(2):
+                qkv[p, 2 * half + h, rows, :] = total[:, h * HD : (h + 1) * HD]
+        add_update(last, 2 * half, 2)
+        for h in (2 * half, 2 * half + 1):
+            send1[4 * h : 4 * h + 4] = update[h].reshape(4, SLICE, HD).astype(BF16)
+        for d in CHIPS_FAR_FIRST:
+            to = lax.rem(chip + d, 8)
+            first_step(half * 8 + to, to * 2 + half).start()
+
+        @pl.when(core != half)
+        def _(half=half):
+            first_step(half * 8 + chip, chip * 2 + half).start()
+
+    got1[col] = send1[mine]
+
+    tile_row = lax.broadcasted_iota(jnp.int32, (TILE, HD), 0)
+    tile = jnp.zeros((TILE, HD), F32)
     for h in range(HEADS):
         high = norm[h].astype(BF16).astype(F32)
         tile = jnp.where(tile_row == h, high, tile)
         tile = jnp.where(tile_row == HEADS + h, norm[h] - high, tile)
-    tile = tile.astype(BF16)
-    for h in range(HEADS):
-        send1[4 * h : 4 * h + 4, 0:SLICE, :] = update[h].reshape(4, SLICE, HD).astype(BF16)
-    for d in range(ROWDEV):
-        send1[d, SLICE:MSG, :] = tile
-
-    def exchange(step, src, dst):
-        for d in FAR_FIRST:
-            pltpu.make_async_remote_copy(
-                src_ref=src.at[lax.rem(col + d, ROWDEV)], dst_ref=dst.at[col],
-                send_sem=s_send.at[step], recv_sem=s_recv.at[step],
-                device_id=in_row(d), device_id_type=MESH,
-            ).start()
-        dst[col] = src[col]
+    tile1[...] = tile.astype(BF16)
+    for d in FAR_FIRST:
+        pltpu.make_async_remote_copy(
+            src_ref=tile1, dst_ref=tiles1.at[col], send_sem=s_send.at[3], recv_sem=s_recv.at[3],
+            device_id=in_row(d), device_id_type=MESH,
+        ).start()
+    tiles1[col] = tile1[...]
 
     def all_of(step, src, dst, count):
         return pltpu.make_async_remote_copy(
@@ -221,43 +241,61 @@
             local[h, mine, :] = (1.0 - share) * dot(probs, v[0:seen, :])
         return carry
 
-    exchange(0, send1, got1)
     keep(0, last, partial_sum(0, last, (0, 1, 2, 3)))
     lax.fori_loop(0, 2, attend, 0)
-    all_of(0, send1, got1, ROWDEV - 1).wait_recv()
+    all_of(0, got1, got1, ROWDEV - 1).wait_recv()
+
+    def second_step(src, dst, step):
+        for d in (2, 1, 3):
+            pltpu.make_async_remote_copy(
+                src_ref=src, dst_ref=dst.at[row], send_sem=s_send.at[step], recv_sem=s_recv.at[step],
+                device_id=in_column(d), device_id_type=MESH,
+            ).start()
+        dst[row] = src[...]
 
     total = got1[0].astype(F32)
     for s in range(1, ROWDEV):
         total = total + got1[s].astype(F32)
     send2[...] = total.astype(BF16)
-    for d in (2, 1, 3):
-        pltpu.make_async_remote_copy(
-            src_ref=send2, dst_ref=got2.at[row], send_sem=s_send.at[1], recv_sem=s_recv.at[1],
-            device_id=in_column(d), device_id_type=MESH,
-        ).start()
-    got2[row] = send2[...]
-    running = jnp.zeros((MSG, HD), F32)
+    second_step(send2, got2, 1)
+    all_of(3, tiles1, tiles1, ROWDEV - 1).wait_recv()
+    total_norm = jnp.zeros((TILE, HD), F32)
+    row_norm = jnp.zeros((TILE, HD), F32)
+    for s in range(ROWDEV):
+        held = tiles1[s].astype(F32)
+        total_norm = total_norm + jnp.where(s < col, held, 0.0)
+        row_norm = row_norm + held
+    tile2[...] = row_norm.astype(BF16)
+    second_step(tile2, tiles2, 4)
+    running = jnp.zeros((SLICE, HD), F32)
     for s in range(ROWDEV):
         prefix[s] = running
         running = running + got1[s].astype(F32)
     lax.fori_loop(2, 3, attend, 0)
     all_of(1, got2, got2, YS - 1).wait_recv()
 
-    offset = jnp.zeros((MSG, HD), F32)
+    offset = jnp.zeros((SLICE, HD), F32)
     for r in range(YS):
         offset = offset + jnp.where(r < row, got2[r].astype(F32), 0.0)
-    for s in range(ROWDEV):
-        send3[s] = (prefix[s, 0:SLICE, :] + offset[0:SLICE, :]).astype(BF16)
-    exchange(2, send3, memory)
+    for d in FAR_FIRST:
+        to = lax.rem(col + d, ROWDEV)
+        send3[to] = (prefix[to] + offset).astype(BF16)
+        pltpu.make_async_remote_copy(
+            src_ref=send3.at[to], dst_ref=memory.at[mine], send_sem=s_send.at[2], recv_sem=s_recv.at[2],
+            device_id=in_row(d), device_id_type=MESH,
+        ).start()
+    memory[mine] = (prefix[col] + offset).astype(BF16)
     lax.fori_loop(3, 4, attend, 0)
 
-    total_norm = prefix[col, SLICE:MSG, :] + offset[SLICE:MSG, :]
+    all_of(4, tiles2, tiles2, YS - 1).wait_recv()
+    for r in range(YS):
+        total_norm = total_norm + jnp.where(r < row, tiles2[r].astype(F32), 0.0)
     for h in range(HEADS):
         normalizer = total_norm[h : h + 1, :] + total_norm[HEADS + h : HEADS + h + 1, :]
         share = jax.nn.sigmoid(jnp.full((8, HD), gate_ref[h], F32))[0:1, :]
         below = jnp.sum(mapped_q[h].astype(F32) * normalizer, axis=-1, keepdims=True)
         scale[h] = share / jnp.maximum(below, 1.0)
-    all_of(2, send3, memory, ROWDEV - 1).wait_recv()
+    all_of(2, memory, memory, ROWDEV - 1).wait_recv()
 
     for h in range(HEADS):
         held = memory[4 * h : 4 * h + 4].reshape(HD, HD)
@@ -270,9 +308,11 @@
             own(c, j).wait_send()
         for copy in to_opposite(c):
             copy.wait_send()
-    all_of(0, send1, got1, ROWDEV - 1).wait_send()
+    all_of(0, got1, got1, ROWDEV - 1).wait_send()
     all_of(1, got2, got2, YS - 1).wait_send()
-    all_of(2, send3, memory, ROWDEV - 1).wait_send()
+    all_of(2, memory, memory, ROWDEV - 1).wait_send()
+    all_of(3, tiles1, tiles1, ROWDEV - 1).wait_send()
+    all_of(4, tiles2, tiles2, YS - 1).wait_send()
 
 
 def per_device(tokens, w_query, w_key, w_value, gate_logit):
@@ -291,22 +331,26 @@
             pltpu.VMEM((3, HEADS, TOK, HD), BF16),
             pltpu.VMEM((2, CHUNKS[-1][1], WIDTH), F32),
             pltpu.VMEM((HEADS, HD, HD), F32),
-            pltpu.VMEM((HEADS, 16, HD), F32),
+            pltpu.VMEM((HEADS, TILE, HD), F32),
             pltpu.VMEM((HEADS, TOK, HD), BF16),
             pltpu.VMEM((HEADS, TOK, HD), F32),
             pltpu.VMEM((HEADS, TOK, HD), F32),
-            pltpu.VMEM((ROWDEV, MSG, HD), BF16),
-            pltpu.VMEM((ROWDEV, MSG, HD), BF16),
-            pltpu.VMEM((MSG, HD), BF16),
-            pltpu.VMEM((YS, MSG, HD), BF16),
-            pltpu.VMEM((ROWDEV, MSG, HD), F32),
+            pltpu.VMEM((ROWDEV, SLICE, HD), BF16),
+            pltpu.VMEM((ROWDEV, SLICE, HD), BF16),
+            pltpu.VMEM((TILE, HD), BF16),
+            pltpu.VMEM((ROWDEV, TILE, HD), BF16),
+            pltpu.VMEM((SLICE, HD), BF16),
+            pltpu.VMEM((YS, SLICE, HD), BF16),
+            pltpu.VMEM((TILE, HD), BF16),
+            pltpu.VMEM((YS, TILE, HD), BF16),
+            pltpu.VMEM((ROWDEV, SLICE, HD), F32),
             pltpu.VMEM((ROWDEV, SLICE, HD), BF16),
             pltpu.VMEM((ROWDEV, SLICE, HD), BF16),
             pltpu.SemaphoreType.DMA((5,)),
             pltpu.SemaphoreType.DMA((4, steps)),
             pltpu.SemaphoreType.DMA((4, steps)),
-            pltpu.SemaphoreType.DMA((3,)),
-            pltpu.SemaphoreType.DMA((3,)),
+            pltpu.SemaphoreType.DMA((5,)),
+            pltpu.SemaphoreType.DMA((5,)),
             pltpu.SemaphoreType.REGULAR((3,)),
         ],
         compiler_params=pltpu.CompilerParams(

time: 64.3 us -> 64 us (level)
  no operation moved by 1% of the time
where the time goes in v3:
time: 64 us; the launch traced here: 63.9 us
  Pallas kernels  62 us (97%)
  local copies, waits for them, and re-layouts  1.87 us (3%)
    pallas_call x1, Pallas kernels, per_device(): pl.pallas_call(kernel, out_shape=jax.ShapeDtypeStruct((TOK, WIDTH), BF16)...  62 us
    unnamed x1, local copies, waits for them, and re-layouts  1.87 us

profile of v3, /device:TPU:1, one launch (start us, length us, event | category | flops | bytes accessed | tf_op | source)
XLA Modules:
  0.0 63.9 jit_solution(1302083904944615147)
XLA Ops:
  0.0 62.0 %shard_map.55 = bf16[512,512]{1,0:T(8,128)(2,1)} custom-call(bf16[512,1024]{1,0:T(8,128)(2,1)} %tok_hbm.1, bf16[4,1024,512]{2,1,0:T(8,128)(2,1)} %bitcast.3, bf16[4,1024,512]{2,1,0:T(8,128)(2,1)} %bitcast.4, bf16[4,1024,512]{2,1,0:T(8,128)(2,1)} %bitcast.5, f32[4]{0:T(128)} %gate_hbm.1), custom_call_target="tpu_custom_call" | custom-call | flops 7400000000 | bytes 15000000 | tf_op jit(solution)/shard_map/pallas_call | solution.py:322
  62.0 1.9 %copy.7 = bf16[512,512]{1,0:T(8,128)(2,1)} copy(bf16[512,512]{1,0:T(8,128)(2,1)} %shard_map.55) | data formatting | bytes 1048576

commit v4 on v3

--- a/solution.py
+++ b/solution.py
@@ -19,7 +19,7 @@
 YS = 4
 SLICE = 32
 TILE = 16
-SIZES = (128, 128, 128, 128)
+SIZES = (128, 160, 128, 96)
 CHUNKS = tuple((sum(SIZES[:i]), n) for i, n in enumerate(SIZES))
 AHEAD = 2
 DIRECT = 0
@@ -159,19 +159,22 @@
             met_all(c)
             if c < 2:
                 meet(c + 1)
+        def begin(p, carry, c=c):
+            acc[p, pl.ds(*CHUNKS[c]), :] = partial_sum(p, c, (0, 1, 2))
+            return carry
+
+        lax.fori_loop(0, 3, begin, 0)
         if c > 0:
             for copy in to_opposite(c - 1):
                 copy.wait_recv()
 
-            def project(p, carry, c=c):
-                keep(p, c - 1, partial_sum(p, c - 1, (0, 1, 2, 3)))
+            def finish(p, carry, c=c):
+                keep(p, c - 1, acc[p, pl.ds(*CHUNKS[c - 1]), :] + partial_sum(p, c - 1, (3,)))
                 return carry
 
-            lax.fori_loop(0, 3, project, 0)
+            lax.fori_loop(0, 3, finish, 0)
             add_update(c - 1)
 
-    for p in (1, 2):
-        acc[p - 1] = partial_sum(p, last, (0, 1, 2))
     for copy in to_opposite(last):
         copy.wait_recv()
     mine = core * 8 + chip
@@ -186,7 +189,7 @@
     for half in range(2):
         columns = pl.ds(half * 256, 256)
         for p in (1, 2):
-            total = acc[p - 1, :, columns] + dot(tok[3, rows, :], weights[p, sources[3], :, columns])
+            total = acc[p, rows, columns] + dot(tok[3, rows, :], weights[p, sources[3], :, columns])
             total = total.astype(BF16)
             for h in range(2):
                 qkv[p, 2 * half + h, rows, :] = total[:, h * HD : (h + 1) * HD]
@@ -241,7 +244,7 @@
             local[h, mine, :] = (1.0 - share) * dot(probs, v[0:seen, :])
         return carry
 
-    keep(0, last, partial_sum(0, last, (0, 1, 2, 3)))
+    keep(0, last, acc[0, rows, :] + partial_sum(0, last, (3,)))
     lax.fori_loop(0, 2, attend, 0)
     all_of(0, got1, got1, ROWDEV - 1).wait_recv()
 
@@ -329,7 +332,7 @@
             pltpu.VMEM((3, 4, DEPTH, WIDTH), BF16),
             pltpu.SMEM((HEADS,), F32),
             pltpu.VMEM((3, HEADS, TOK, HD), BF16),
-            pltpu.VMEM((2, CHUNKS[-1][1], WIDTH), F32),
+            pltpu.VMEM((3, TOK, WIDTH), F32),
             pltpu.VMEM((HEADS, HD, HD), F32),
             pltpu.VMEM((HEADS, TILE, HD), F32),
             pltpu.VMEM((HEADS, TOK, HD), BF16),

time: 64 us -> 62.9 us (0.983)
  Pallas kernels: 62 us -> 60.9 us
    pallas_call x1, Pallas kernels: 62 us -> 60.9 us  [per_device(): pl.pallas_call(kernel, out_shape=jax.ShapeDtypeStruct((TOK, WIDTH), BF16)...]
where the time goes in v4:
time: 62.9 us; the launch traced here: 62.8 us
  Pallas kernels  60.9 us (97%)
  local copies, waits for them, and re-layouts  1.87 us (3%)
    pallas_call x1, Pallas kernels, per_device(): pl.pallas_call(kernel, out_shape=jax.ShapeDtypeStruct((TOK, WIDTH), BF16)...  60.9 us
    unnamed x1, local copies, waits for them, and re-layouts  1.87 us

profile of v4, /device:TPU:1, one launch (start us, length us, event | category | flops | bytes accessed | tf_op | source)
XLA Modules:
  0.0 62.8 jit_solution(17463255176294971963)
XLA Ops:
  0.0 60.9 %shard_map.55 = bf16[512,512]{1,0:T(8,128)(2,1)} custom-call(bf16[512,1024]{1,0:T(8,128)(2,1)} %tok_hbm.1, bf16[4,1024,512]{2,1,0:T(8,128)(2,1)} %bitcast.3, bf16[4,1024,512]{2,1,0:T(8,128)(2,1)} %bitcast.4, bf16[4,1024,512]{2,1,0:T(8,128)(2,1)} %bitcast.5, f32[4]{0:T(128)} %gate_hbm.1), custom_call_target="tpu_custom_call" | custom-call | flops 7400000000 | bytes 15000000 | tf_op jit(solution)/shard_map/pallas_call | solution.py:325
  60.9 1.9 %copy.7 = bf16[512,512]{1,0:T(8,128)(2,1)} copy(bf16[512,512]{1,0:T(8,128)(2,1)} %shard_map.55) | data formatting | bytes 1048576

commit v5 on v4

--- a/solution.py
+++ b/solution.py
@@ -24,6 +24,7 @@
 AHEAD = 2
 DIRECT = 0
 FAR_FIRST = (8, 7, 9, 6, 10, 5, 11, 4, 12, 3, 13, 2, 14, 1, 15)
+TARGETS = (0, 1, 2, 3, 4, 5, 6, 7, 14, 15, 8, 9, 12, 13, 10, 11)
 CHIPS_FAR_FIRST = (4, 3, 5, 2, 6, 1, 7)
 
 
@@ -38,7 +39,7 @@
 def kernel(
     tok_hbm, wq_hbm, wk_hbm, wv_hbm, gate_hbm, out_ref,
     tok, weights, gate_ref, qkv, acc, update, norm, mapped_q, local, scale,
-    send1, got1, tile1, tiles1, send2, got2, tile2, tiles2, prefix, send3, memory,
+    send1, got1, tile1, tiles1, send2, got2, tile2, tiles2, prefix, offset2, offset_tile, send3, memory,
     load_sem, x_send, x_recv, s_send, s_recv, met,
 ):
     me = lax.axis_index("ctx")
@@ -249,12 +250,24 @@
     all_of(0, got1, got1, ROWDEV - 1).wait_recv()
 
     def second_step(src, dst, step):
-        for d in (2, 1, 3):
-            pltpu.make_async_remote_copy(
-                src_ref=src, dst_ref=dst.at[row], send_sem=s_send.at[step], recv_sem=s_recv.at[step],
-                device_id=in_column(d), device_id_type=MESH,
-            ).start()
-        dst[row] = src[...]
+        for to in range(1, YS):
+
+            @pl.when(row < to)
+            def _(to=to):
+                pltpu.make_async_remote_copy(
+                    src_ref=src, dst_ref=dst.at[row],
+                    send_sem=s_send.at[step], recv_sem=s_recv.at[step],
+                    device_id={"ctx": to * ROWDEV + col}, device_id_type=MESH,
+                ).start()
+
+    def earlier_rows(dst, step, into):
+        into[...] = jnp.zeros_like(into)
+        for n in range(1, YS):
+
+            @pl.when(row == n)
+            def _(n=n):
+                all_of(step, dst, dst, n).wait_recv()
+                into[...] = sum(dst[r].astype(F32) for r in range(n))
 
     total = got1[0].astype(F32)
     for s in range(1, ROWDEV):
@@ -275,24 +288,25 @@
         prefix[s] = running
         running = running + got1[s].astype(F32)
     lax.fori_loop(2, 3, attend, 0)
-    all_of(1, got2, got2, YS - 1).wait_recv()
-
-    offset = jnp.zeros((SLICE, HD), F32)
-    for r in range(YS):
-        offset = offset + jnp.where(r < row, got2[r].astype(F32), 0.0)
-    for d in FAR_FIRST:
-        to = lax.rem(col + d, ROWDEV)
+
+    earlier_rows(got2, 1, offset2)
+    offset = offset2[...]
+    for to in TARGETS:
         send3[to] = (prefix[to] + offset).astype(BF16)
-        pltpu.make_async_remote_copy(
-            src_ref=send3.at[to], dst_ref=memory.at[mine], send_sem=s_send.at[2], recv_sem=s_recv.at[2],
-            device_id=in_row(d), device_id_type=MESH,
-        ).start()
+
+        @pl.when(col != to)
+        def _(to=to):
+            pltpu.make_async_remote_copy(
+                src_ref=send3.at[to], dst_ref=memory.at[mine],
+                send_sem=s_send.at[2], recv_sem=s_recv.at[2],
+                device_id={"ctx": row * ROWDEV + to}, device_id_type=MESH,
+            ).start()
+
     memory[mine] = (prefix[col] + offset).astype(BF16)
     lax.fori_loop(3, 4, attend, 0)
 
-    all_of(4, tiles2, tiles2, YS - 1).wait_recv()
-    for r in range(YS):
-        total_norm = total_norm + jnp.where(r < row, tiles2[r].astype(F32), 0.0)
+    earlier_rows(tiles2, 4, offset_tile)
+    total_norm = total_norm + offset_tile[...]
     for h in range(HEADS):
         normalizer = total_norm[h : h + 1, :] + total_norm[HEADS + h : HEADS + h + 1, :]
         share = jax.nn.sigmoid(jnp.full((8, HD), gate_ref[h], F32))[0:1, :]
@@ -312,10 +326,14 @@
         for copy in to_opposite(c):
             copy.wait_send()
     all_of(0, got1, got1, ROWDEV - 1).wait_send()
-    all_of(1, got2, got2, YS - 1).wait_send()
     all_of(2, memory, memory, ROWDEV - 1).wait_send()
     all_of(3, tiles1, tiles1, ROWDEV - 1).wait_send()
-    all_of(4, tiles2, tiles2, YS - 1).wait_send()
+    for n in range(YS - 1):
+
+        @pl.when(row == n)
+        def _(n=n):
+            all_of(1, got2, got2, YS - 1 - n).wait_send()
+            all_of(4, tiles2, tiles2, YS - 1 - n).wait_send()
 
 
 def per_device(tokens, w_query, w_key, w_value, gate_logit):
@@ -347,6 +365,8 @@
             pltpu.VMEM((TILE, HD), BF16),
             pltpu.VMEM((YS, TILE, HD), BF16),
             pltpu.VMEM((ROWDEV, SLICE, HD), F32),
+            pltpu.VMEM((SLICE, HD), F32),
+            pltpu.VMEM((TILE, HD), F32),
             pltpu.VMEM((ROWDEV, SLICE, HD), BF16),
             pltpu.VMEM((ROWDEV, SLICE, HD), BF16),
             pltpu.SemaphoreType.DMA((5,)),

time: 62.9 us -> 61.2 us (0.973)
  Pallas kernels: 60.9 us -> 59.2 us
    pallas_call x1, Pallas kernels: 60.9 us -> 59.2 us  [per_device(): pl.pallas_call(kernel, out_shape=jax.ShapeDtypeStruct((TOK, WIDTH), BF16)...]
where the time goes in v5:
time: 61.2 us; the launch traced here: 61.1 us
  Pallas kernels  59.2 us (97%)
  local copies, waits for them, and re-layouts  1.87 us (3%)
    pallas_call x1, Pallas kernels, per_device(): pl.pallas_call(kernel, out_shape=jax.ShapeDtypeStruct((TOK, WIDTH), BF16)...  59.2 us
    unnamed x1, local copies, waits for them, and re-layouts  1.87 us

profile of v5, /device:TPU:1, one launch (start us, length us, event | category | flops | bytes accessed | tf_op | source)
XLA Modules:
  0.0 61.1 jit_solution(8773920857141332712)
XLA Ops:
  0.0 59.2 %shard_map.55 = bf16[512,512]{1,0:T(8,128)(2,1)} custom-call(bf16[512,1024]{1,0:T(8,128)(2,1)} %tok_hbm.1, bf16[4,1024,512]{2,1,0:T(8,128)(2,1)} %bitcast.3, bf16[4,1024,512]{2,1,0:T(8,128)(2,1)} %bitcast.4, bf16[4,1024,512]{2,1,0:T(8,128)(2,1)} %bitcast.5, f32[4]{0:T(128)} %gate_hbm.1), custom_call_target="tpu_custom_call" | custom-call | flops 7400000000 | bytes 15000000 | tf_op jit(solution)/shard_map/pallas_call | solution.py:343
  59.2 1.9 %copy.7 = bf16[512,512]{1,0:T(8,128)(2,1)} copy(bf16[512,512]{1,0:T(8,128)(2,1)} %shard_map.55) | data formatting | bytes 1048576

commit v6 on v5

--- a/solution.py
+++ b/solution.py
@@ -287,7 +287,6 @@
     for s in range(ROWDEV):
         prefix[s] = running
         running = running + got1[s].astype(F32)
-    lax.fori_loop(2, 3, attend, 0)
 
     earlier_rows(got2, 1, offset2)
     offset = offset2[...]
@@ -303,7 +302,7 @@
             ).start()
 
     memory[mine] = (prefix[col] + offset).astype(BF16)
-    lax.fori_loop(3, 4, attend, 0)
+    lax.fori_loop(2, 4, attend, 0)
 
     earlier_rows(tiles2, 4, offset_tile)
     total_norm = total_norm + offset_tile[...]

time: 61.2 us -> 59.8 us (0.977)
  Pallas kernels: 59.2 us -> 57.8 us
    pallas_call x1, Pallas kernels: 59.2 us -> 57.8 us  [per_device(): pl.pallas_call(kernel, out_shape=jax.ShapeDtypeStruct((TOK, WIDTH), BF16)...]
where the time goes in v6:
time: 59.8 us; the launch traced here: 59.6 us
  Pallas kernels  57.8 us (97%)
  local copies, waits for them, and re-layouts  1.87 us (3%)
    pallas_call x1, Pallas kernels, per_device(): pl.pallas_call(kernel, out_shape=jax.ShapeDtypeStruct((TOK, WIDTH), BF16)...  57.8 us
    unnamed x1, local copies, waits for them, and re-layouts  1.87 us

profile of v6, /device:TPU:1, one launch (start us, length us, event | category | flops | bytes accessed | tf_op | source)
XLA Modules:
  0.0 59.6 jit_solution(16281679621605358839)
XLA Ops:
  0.0 57.8 %shard_map.55 = bf16[512,512]{1,0:T(8,128)(2,1)} custom-call(bf16[512,1024]{1,0:T(8,128)(2,1)} %tok_hbm.1, bf16[4,1024,512]{2,1,0:T(8,128)(2,1)} %bitcast.3, bf16[4,1024,512]{2,1,0:T(8,128)(2,1)} %bitcast.4, bf16[4,1024,512]{2,1,0:T(8,128)(2,1)} %bitcast.5, f32[4]{0:T(128)} %gate_hbm.1), custom_call_target="tpu_custom_call" | custom-call | flops 7400000000 | bytes 15000000 | tf_op jit(solution)/shard_map/pallas_call | solution.py:342
  57.8 1.9 %copy.7 = bf16[512,512]{1,0:T(8,128)(2,1)} copy(bf16[512,512]{1,0:T(8,128)(2,1)} %shard_map.55) | data formatting | bytes 1048576

commit v7 on v6

--- a/solution.py
+++ b/solution.py
@@ -274,6 +274,25 @@
         total = total + got1[s].astype(F32)
     send2[...] = total.astype(BF16)
     second_step(send2, got2, 1)
+    running = jnp.zeros((SLICE, HD), F32)
+    for s in range(ROWDEV):
+        prefix[s] = running
+        running = running + got1[s].astype(F32)
+
+    earlier_rows(got2, 1, offset2)
+    offset = offset2[...]
+    for to in TARGETS:
+        send3[to] = (prefix[to] + offset).astype(BF16)
+
+        @pl.when(col != to)
+        def _(to=to):
+            pltpu.make_async_remote_copy(
+                src_ref=send3.at[to], dst_ref=memory.at[mine],
+                send_sem=s_send.at[2], recv_sem=s_recv.at[2],
+                device_id={"ctx": row * ROWDEV + to}, device_id_type=MESH,
+            ).start()
+
+    memory[mine] = (prefix[col] + offset).astype(BF16)
     all_of(3, tiles1, tiles1, ROWDEV - 1).wait_recv()
     total_norm = jnp.zeros((TILE, HD), F32)
     row_norm = jnp.zeros((TILE, HD), F32)
@@ -283,25 +302,6 @@
         row_norm = row_norm + held
     tile2[...] = row_norm.astype(BF16)
     second_step(tile2, tiles2, 4)
-    running = jnp.zeros((SLICE, HD), F32)
-    for s in range(ROWDEV):
-        prefix[s] = running
-        running = running + got1[s].astype(F32)
-
-    earlier_rows(got2, 1, offset2)
-    offset = offset2[...]
-    for to in TARGETS:
-        send3[to] = (prefix[to] + offset).astype(BF16)
-
-        @pl.when(col != to)
-        def _(to=to):
-            pltpu.make_async_remote_copy(
-                src_ref=send3.at[to], dst_ref=memory.at[mine],
-                send_sem=s_send.at[2], recv_sem=s_recv.at[2],
-                device_id={"ctx": row * ROWDEV + to}, device_id_type=MESH,
-            ).start()
-
-    memory[mine] = (prefix[col] + offset).astype(BF16)
     lax.fori_loop(2, 4, attend, 0)
 
     earlier_rows(tiles2, 4, offset_tile)

time: 59.8 us -> 59.7 us (level)
  Pallas kernels: 57.8 us -> 57.1 us
    pallas_call x1, Pallas kernels: 57.8 us -> 57.1 us  [per_device(): pl.pallas_call(kernel, out_shape=jax.ShapeDtypeStruct((TOK, WIDTH), BF16)...]
where the time goes in v7:
time: 59.7 us; the launch traced here: 59 us
  Pallas kernels  57.1 us (96%)
  local copies, waits for them, and re-layouts  1.87 us (3%)
    pallas_call x1, Pallas kernels, per_device(): pl.pallas_call(kernel, out_shape=jax.ShapeDtypeStruct((TOK, WIDTH), BF16)...  57.1 us
    unnamed x1, local copies, waits for them, and re-layouts  1.87 us

profile of v7, /device:TPU:1, one launch (start us, length us, event | category | flops | bytes accessed | tf_op | source)
XLA Modules:
  0.0 59.0 jit_solution(6632390810680792781)
XLA Ops:
  0.0 57.1 %shard_map.55 = bf16[512,512]{1,0:T(8,128)(2,1)} custom-call(bf16[512,1024]{1,0:T(8,128)(2,1)} %tok_hbm.1, bf16[4,1024,512]{2,1,0:T(8,128)(2,1)} %bitcast.3, bf16[4,1024,512]{2,1,0:T(8,128)(2,1)} %bitcast.4, bf16[4,1024,512]{2,1,0:T(8,128)(2,1)} %bitcast.5, f32[4]{0:T(128)} %gate_hbm.1), custom_call_target="tpu_custom_call" | custom-call | flops 7400000000 | bytes 15000000 | tf_op jit(solution)/shard_map/pallas_call | solution.py:342
  57.1 1.9 %copy.7 = bf16[512,512]{1,0:T(8,128)(2,1)} copy(bf16[512,512]{1,0:T(8,128)(2,1)} %shard_map.55) | data formatting | bytes 1048576

commit v8 on v7

--- a/solution.py
+++ b/solution.py
@@ -269,15 +269,12 @@
                 all_of(step, dst, dst, n).wait_recv()
                 into[...] = sum(dst[r].astype(F32) for r in range(n))
 
-    total = got1[0].astype(F32)
-    for s in range(1, ROWDEV):
-        total = total + got1[s].astype(F32)
-    send2[...] = total.astype(BF16)
-    second_step(send2, got2, 1)
     running = jnp.zeros((SLICE, HD), F32)
     for s in range(ROWDEV):
         prefix[s] = running
         running = running + got1[s].astype(F32)
+    send2[...] = running.astype(BF16)
+    second_step(send2, got2, 1)
 
     earlier_rows(got2, 1, offset2)
     offset = offset2[...]

time: 59.7 us -> 59.7 us (level)
  no operation moved by 1% of the time
where the time goes in v8:
time: 59.7 us; the launch traced here: 59 us
  Pallas kernels  57.1 us (96%)
  local copies, waits for them, and re-layouts  1.87 us (3%)
    pallas_call x1, Pallas kernels, per_device(): pl.pallas_call(kernel, out_shape=jax.ShapeDtypeStruct((TOK, WIDTH), BF16)...  57.1 us
    unnamed x1, local copies, waits for them, and re-layouts  1.87 us

profile of v8, /device:TPU:1, one launch (start us, length us, event | category | flops | bytes accessed | tf_op | source)
XLA Modules:
  0.0 59.0 jit_solution(2529882040482086971)
XLA Ops:
  0.0 57.1 %shard_map.55 = bf16[512,512]{1,0:T(8,128)(2,1)} custom-call(bf16[512,1024]{1,0:T(8,128)(2,1)} %tok_hbm.1, bf16[4,1024,512]{2,1,0:T(8,128)(2,1)} %bitcast.3, bf16[4,1024,512]{2,1,0:T(8,128)(2,1)} %bitcast.4, bf16[4,1024,512]{2,1,0:T(8,128)(2,1)} %bitcast.5, f32[4]{0:T(128)} %gate_hbm.1), custom_call_target="tpu_custom_call" | custom-call | flops 7400000000 | bytes 15000000 | tf_op jit(solution)/shard_map/pallas_call | solution.py:339
  57.1 1.9 %copy.7 = bf16[512,512]{1,0:T(8,128)(2,1)} copy(bf16[512,512]{1,0:T(8,128)(2,1)} %shard_map.55) | data formatting | bytes 1048576
